TPU v7x, 128 devices: a whole 4x4x4 slice. The times are simulated.
128 devices in a mesh: fsdp: 32 (over z, x, core), feat: 4 (over y).
Axes of the slice: x: 4, y: 4, z: 4, core: 2. Of those that a mesh axis runs over, the one named last changes fastest.
Arguments:
- table_cells: bfloat16 [1536, 256, 192], P(('fsdp', 'feat'))
- attn_weights: bfloat16 [8, 192, 192], P(None, 'fsdp')
- hidden_up_weight: bfloat16 [192, 384], P('fsdp'), may hold values from -0.4375 to 0.4375
- hidden_down_weight: bfloat16 [384, 192], P('fsdp'), may hold values from -0.3125 to 0.3125
- norm_gains: float32 [3, 192], replicated, may hold values from 0.25 to 1.75
- train_count: int32 [1], replicated, may hold values from 384 to 1152
- feature_count: int32 [1], replicated, may hold values from 128 to 256
Outputs:
- layer_out: bfloat16 [1536, 256, 192], P(('fsdp', 'feat'))
Inputs may be any that keep to these rules, and one draw needn't show every extreme that they name: Rows 0 to train_count - 1 are the training rows. Features 0 to feature_count - 1 are real, the others padding.
All inputs are finite; a program needn't handle non-finite values.
Results may differ from a plain program's by a relative error of at most 0.012.
The roundings to bfloat16 on the way count: a program that leaves them out, or rounds other values in their place, can miss the bound.
Values may be sent and summed in bfloat16 or wider, within the bound.
A program may use at most 128 MiB of HBM per device.

v0:
```python
import jax
import jax.numpy as jnp
from jax import lax
from jax.sharding import PartitionSpec as P

HEADS = 6
EPS = 1e-05
NEGATIVE = -1e30


def normalize(value_rows, gain):
    floats = value_rows.astype(jnp.float32)
    average = jnp.mean(floats, axis=-1, keepdims=True)
    centered = floats - average
    variance = jnp.mean(centered * centered, axis=-1, keepdims=True)
    return (centered * lax.rsqrt(variance + EPS) * gain).astype(jnp.bfloat16)


def softmax_rows(scores, live):
    masked = jnp.where(live, scores, NEGATIVE)
    row_maximum = jnp.max(masked, axis=-1, keepdims=True)
    exponent = jnp.exp(masked - row_maximum)
    return (exponent / jnp.sum(exponent, axis=-1, keepdims=True)).astype(jnp.bfloat16)


def project(normed, weight):
    model_width = normed.shape[-1]
    product = jnp.dot(normed.reshape(-1, model_width), weight, preferred_element_type=jnp.float32)
    return product.astype(jnp.bfloat16).reshape(normed.shape[:-1] + (weight.shape[1],))


def output_proj(attended_rows, residual, weight):
    model_width = attended_rows.shape[-1]
    product = jnp.dot(
        attended_rows.reshape(-1, model_width), weight, preferred_element_type=jnp.float32
    )
    return (residual.astype(jnp.float32) + product.reshape(residual.shape)).astype(jnp.bfloat16)


def feature_attention(table_cells, normed, weights, feat_live):
    model_width = normed.shape[-1]
    head_size = model_width // HEADS
    queries = project(normed, weights[0])
    keys = project(normed, weights[1])
    value_rows = project(normed, weights[2])
    outputs = []
    for index_head in range(HEADS):
        training_extent = slice(index_head * head_size, (index_head + 1) * head_size)
        scores = jnp.einsum(
            "rqe,rke->rqk",
            queries[..., training_extent],
            keys[..., training_extent],
            preferred_element_type=jnp.float32,
        ) * head_size ** (-0.5)
        attention_probabilities = softmax_rows(scores, feat_live[None, None, :])
        outputs.append(
            jnp.einsum(
                "rqk,rke->rqe",
                attention_probabilities,
                value_rows[..., training_extent],
                preferred_element_type=jnp.float32,
            ).astype(jnp.bfloat16)
        )
    return output_proj(jnp.concatenate(outputs, axis=-1), table_cells, weights[3])


def sample_attention(column_block, normed, weights, row_live):
    all_rows, feat_here, model_width = normed.shape
    head_size = model_width // HEADS
    queries = project(normed, weights[4])
    keys = project(normed, weights[5])
    value_rows = project(normed, weights[6])
    block_count = max(1, all_rows // 512)
    block_rows = all_rows // block_count
    query_blocks = queries.reshape(block_count, block_rows, feat_here, model_width)

    def one_block(query_block):
        outputs = []
        for index_head in range(HEADS):
            training_extent = slice(index_head * head_size, (index_head + 1) * head_size)
            scores = jnp.einsum(
                "vsg,psg->svp",
                query_block[..., training_extent],
                keys[..., training_extent],
                preferred_element_type=jnp.float32,
            ) * head_size ** (-0.5)
            attention_probabilities = softmax_rows(scores, row_live[None, None, :])
            outputs.append(
                jnp.einsum(
                    "tdj,jtn->dtn",
                    attention_probabilities,
                    value_rows[..., training_extent],
                    preferred_element_type=jnp.float32,
                ).astype(jnp.bfloat16)
            )
        return jnp.concatenate(outputs, axis=-1)

    attended_rows = lax.map(one_block, query_blocks).reshape(all_rows, feat_here, model_width)
    return output_proj(attended_rows, column_block, weights[7])


def feed_forward(value_rows, gain, w_in, w_out):
    model_width = value_rows.shape[-1]
    normed = normalize(value_rows, gain)
    hidden = jnp.dot(normed.reshape(-1, model_width), w_in, preferred_element_type=jnp.float32)
    activated = jax.nn.gelu(hidden).astype(jnp.bfloat16)
    result = value_rows.astype(jnp.float32) + jnp.dot(
        activated, w_out, preferred_element_type=jnp.float32
    ).reshape(value_rows.shape)
    return result.astype(jnp.bfloat16)


def local(
    table_cells,
    attn_weights,
    hidden_up_weight,
    hidden_down_weight,
    norm_gains,
    train_count,
    feature_count,
):
    weights, w_in, w_out = (
        lax.all_gather(attn_weights, "fsdp", axis=1, tiled=True),
        lax.all_gather(hidden_up_weight, "fsdp", axis=0, tiled=True),
        lax.all_gather(hidden_down_weight, "fsdp", axis=0, tiled=True),
    )
    feat_live = jnp.arange(table_cells.shape[1]) < feature_count[0]
    normed_one = normalize(table_cells, norm_gains[0])
    mixed_rows = feature_attention(table_cells, normed_one, weights, feat_live)
    fsdp_size = lax.axis_size("fsdp")
    groups = lax.axis_size("feat")
    row_dev, feat_total, model_width = table_cells.shape
    devices_all = fsdp_size * groups
    all_rows = row_dev * devices_all
    train_limit = train_count[0]
    row_index = jnp.arange(all_rows)
    split_cells = mixed_rows.reshape(row_dev, devices_all, feat_total // devices_all, model_width)
    column_block = lax.all_to_all(
        split_cells, ("fsdp", "feat"), split_axis=1, concat_axis=0, tiled=True
    )
    rows_here, single, feat_here, width_here = column_block.shape
    owner_column_block = column_block.reshape(rows_here, feat_here, width_here)
    normed_two = normalize(owner_column_block, norm_gains[1])
    sampled = sample_attention(owner_column_block, normed_two, weights, row_index < train_limit)
    at_owners = sampled.reshape(rows_here, single, feat_here, width_here)
    returned = lax.all_to_all(at_owners, ("fsdp", "feat"), split_axis=0, concat_axis=1, tiled=True)
    returned = returned.reshape(row_dev, feat_total, model_width)
    returned = feed_forward(returned, norm_gains[2], w_in, w_out)
    return returned


def solution(mesh):
    in_specs = (
        P(("fsdp", "feat"), None, None),
        P(None, "fsdp", None),
        P("fsdp", None),
        P("fsdp", None),
        P(),
        P(),
        P(),
    )
    out_specs = P(("fsdp", "feat"), None, None)
    return jax.shard_map(local, mesh=mesh, in_specs=in_specs, out_specs=out_specs, check_vma=False)
```

profile of v0, /device:TPU:1, one launch (start us, length us, event | category | flops | bytes accessed | tf_op | source)
XLA Modules:
  0.0 370.8 jit_solution(5374347418670035218)
XLA Ops:
  0.0 27.7 %all_gather.9 = bf16[8,192,192]{2,0,1:T(8,128)(2,1)S(1)} all-gather(bf16[8,6,192]{2,0,1:T(8,128)(2,1)} %param.10), channel_id=1, replica_groups=mesh['fsdp'=32,'feat'=4] {'fsdp'}, dimensions={1}, use_global_device_ids=true | all-gather | bytes 608256 | tf_op jit(solution)/shard_map/all_gather | solution.py:123
  27.7 2.2 fusion.415
  37.6 2.5 convolution_convert_fusion.3
  40.0 2.8 reshape.232
  44.0 3.1 fusion.413
  47.1 3.9 %fusion.417 = (f32[12,256]{1,0:T(8,128)S(1)}, f32[12,256,256]{1,2,0:T(8,128)}) fusion(pred[256]{0:T(512)(128)(4,1)S(1)} %iota_compare_fusion.1, bf16[12,256,32]{1,0,2:T(8,128)(2,1)} %get-tuple-element.136, bf16[12,256,32]{1,0,2:T(8,128)(2,1)} %get-tuple-element.106), kind=kOutput, calls=%fused_computation.353 | convolution fusion | flops 53477632 | bytes 3551488 | tf_op jit(solution)/shard_map/sub | solution.py:22
  51.0 4.0 %fusion.426 = (f32[12,256]{1,0:T(8,128)S(1)}, f32[12,256,256]{1,2,0:T(8,128)}) fusion(pred[256]{0:T(512)(128)(4,1)S(1)} %iota_compare_fusion.1, bf16[12,256,32]{1,0,2:T(8,128)(2,1)} %get-tuple-element.137, bf16[12,256,32]{1,0,2:T(8,128)(2,1)} %get-tuple-element.105), kind=kOutput, calls=%fused_computation.354 | convolution fusion | flops 53477632 | bytes 3551488 | tf_op jit(solution)/shard_map/sub | solution.py:22
  55.0 4.0 %fusion.435 = (f32[12,256]{1,0:T(8,128)S(1)}, f32[12,256,256]{1,2,0:T(8,128)}) fusion(pred[256]{0:T(512)(128)(4,1)S(1)} %iota_compare_fusion.1, bf16[12,256,32]{1,0,2:T(8,128)(2,1)} %get-tuple-element.138, bf16[12,256,32]{1,0,2:T(8,128)(2,1)} %get-tuple-element.104), kind=kOutput, calls=%fused_computation.355 | convolution fusion | flops 53477632 | bytes 3551488 | tf_op jit(solution)/shard_map/sub | solution.py:22
  59.0 2.9 fusion.444
  61.8 2.9 fusion.453
  64.7 2.9 fusion.462
  67.6 2.4 fusion.274
  82.7 2.2 copy.182
  84.9 7.2 %all-to-all-start = ((bf16[12,128,2,192]{3,2,0,1:T(2,128)(2,1)}), bf16[12,128,2,192]{3,2,0,1:T(2,128)(2,1)S(1)}, u32[]{:S(2)}, u32[]{:S(2)}) async-start(bf16[12,128,2,192]{3,2,0,1:T(2,128)(2,1)} %copy.182), calls=%async_computation | async-start | bytes 3145728 | tf_op jit(solution)/shard_map/all_to_all | solution.py:138
  92.9 24.1 %all-to-all-done = bf16[12,128,2,192]{3,2,0,1:T(2,128)(2,1)S(1)} async-done(((bf16[12,128,2,192]{3,2,0,1:T(2,128)(2,1)}), bf16[12,128,2,192]{3,2,0,1:T(2,128)(2,1)S(1)}, u32[]{:S(2)}, u32[]{:S(2)}) %all-to-all-start) | async-done | bytes 1179680 | tf_op jit(solution)/shard_map/all_to_all | solution.py:138
  118.9 4.0 %multiply_reduce_fusion.1 = f32[128,12,2]{2,1,0:T(8,128)S(1)} fusion(bf16[12,128,2,192]{3,2,0,1:T(2,128)(2,1)S(1)} %all-to-all-done, f32[128,12,2]{2,1,0:T(8,128)S(1)} %broadcast_multiply_fusion.1), kind=kLoop, calls=%fused_computation.190 | loop fusion | flops 2356224 | bytes 1204224 | tf_op jit(solution)/shard_map/reduce_sum | solution.py:15
  123.1 3.9 %multiply_convert_fusion.1 = bf16[128,12,1,2,192]{4,3,1,0,2:T(2,128)(2,1)S(1)} fusion(bf16[12,128,2,192]{3,2,0,1:T(2,128)(2,1)S(1)} %all-to-all-done, f32[192]{0:T(256)S(1)} %bitcast.148, f32[128,12,2]{2,1,0:T(8,128)S(1)} %add_rsqrt_fusion.1, f32[128,12,2]{2,1,0:T(8,128)S(1)} %broadcast_multiply_fusion.1), kind=kLoop, calls=%fused_computation.189 | loop fusion | flops 2949120 | bytes 2384640 | tf_op jit(solution)/shard_map/convert_element_type | solution.py:16
  131.9 2.2 reshape.234
  134.0 4.9 %copy.190 = bf16[1536,2,192]{0,2,1:T(8,128)(2,1)} copy(bf16[1536,2,192]{2,1,0:T(2,128)(2,1)} %reshape.234) | data formatting | bytes 2359296
  142.3 2.2 reshape.235
  144.4 4.9 %copy.191 = bf16[1536,2,192]{0,2,1:T(8,128)(2,1)} copy(bf16[1536,2,192]{2,1,0:T(2,128)(2,1)} %reshape.235) | data formatting | bytes 2359296
  152.6 105.7 %while.11 = (s32[]{:T(128)}, bf16[3,512,2,192]{1,3,2,0:T(8,128)(2,1)}, bf16[3,512,2,192]{1,3,2,0:T(8,128)(2,1)S(1)}, bf16[1536,2,192]{0,2,1:T(8,128)(2,1)}, bf16...) while((s32[]{:T(128)}, bf16[3,512,2,192]{1,3,2,0:T(8,128)(2,1)}, ...), condition=%wide.region_29.30_spmd.clone, body=%wide.region_16.29_spmd.clone.sunk | while | flops 1897096704 | bytes 11085937 | solution.py:98
  153.5 3.1 fusion.553
  156.7 3.3 fusion.554
  162.1 3.3 fusion.556
  165.4 2.1 fusion.557
  167.5 3.3 fusion.558
  172.9 3.3 fusion.560
  176.2 2.1 fusion.561
  178.4 3.3 fusion.562
  183.8 3.3 fusion.564
  188.6 3.1 fusion.553
  191.7 3.3 fusion.554
  197.1 3.3 fusion.556
  200.4 2.1 fusion.557
  202.6 3.3 fusion.558
  208.0 3.3 fusion.560
  211.3 2.1 fusion.561
  213.4 3.3 fusion.562
  216.7 2.1 fusion.563
  218.9 3.3 fusion.564
  223.6 3.1 fusion.553
  226.8 3.3 fusion.554
  230.0 2.1 fusion.555
  232.2 3.3 fusion.556
  235.5 2.1 fusion.557
  237.6 3.3 fusion.558
  243.0 3.3 fusion.560
  246.3 2.1 fusion.561
  248.5 3.3 fusion.562
  253.9 3.3 fusion.564
  258.4 2.5 copy.239
  262.0 3.3 copy.194
  265.3 2.5 fusion.223
  267.8 2.9 copy.195
  270.7 3.9 %all-to-all-start.1 = ((bf16[1536,1,2,192]{3,2,1,0:T(2,128)(2,1)}), bf16[1536,1,2,192]{3,2,1,0:T(2,128)(2,1)S(1)}, u32[]{:S(2)}, u32[]{:S(2)}) async-start(bf16[1536,1,2,192]{3,2,1,0:T(2,128)(2,1)} %copy.195), calls=%async_computation.1 | async-start | bytes 3145728 | tf_op jit(solution)/shard_map/all_to_all | solution.py:146
  274.6 39.1 %all-gather.1 = bf16[32,12,192]{2,1,0:T(8,128)(2,1)S(1)} all-gather(bf16[1,12,192]{2,1,0:T(8,128)(2,1)S(1)} %bitcast.145), channel_id=1, replica_groups=mesh['fsdp'=32,'feat'=4] {'fsdp'}, dimensions={0}, use_global_device_ids=true | all-gather | bytes 152064 | tf_op jit(solution)/shard_map/all_gather | solution.py:125
  313.8 22.8 %all-gather = bf16[32,6,384]{2,1,0:T(8,128)(2,1)S(1)} all-gather(bf16[1,6,384]{2,1,0:T(8,128)(2,1)S(1)} %bitcast.146), channel_id=1, replica_groups=mesh['fsdp'=32,'feat'=4] {'fsdp'}, dimensions={0}, use_global_device_ids=true | all-gather | bytes 152064 | tf_op jit(solution)/shard_map/all_gather | solution.py:124
  339.6 5.1 %multiply_reduce_fusion = f32[12,128,2]{2,0,1:T(8,128)} fusion(bf16[128,12,1,2,192]{4,3,1,0,2:T(2,128)(2,1)S(1)} %bitcast.137, f32[12,128,2]{2,0,1:T(8,128)S(1)} %broadcast_multiply_fusion), kind=kLoop, calls=%fused_computation.188 | loop fusion | flops 2356224 | bytes 1204224 | tf_op jit(solution)/shard_map/reduce_sum | solution.py:15
  347.3 3.4 reshape.240
  350.8 3.4 reshape.239
  359.9 2.2 copy.203
  362.0 5.6 %fusion.235 = f32[3072,192]{0,1:T(8,128)} fusion(bf16[384,192]{1,0:T(8,128)(2,1)S(1)} %reshape.249, bf16[192,384]{1,0:T(8,128)(2,1)S(1)} %reshape.247, f32[3072,192]{1,0:T(8,128)} %reshape.240, f32[192]{0:T(256)S(1)} %bitcast.149, f32[3072]{0:T(1024)S(1)} %rsqrt.30, f32[3072]{0:T(1024)S(1)} %div.133), kind=kOutput, calls=%fused_computation.226 | convolution fusion | flops 918945792 | bytes 5038848 | tf_op jit(solution)/shard_map/dot_general | solution.py:107
  367.6 2.9 fusion.234
  (119 shorter events, 66.8 us)
Async XLA Ops:
  0.0 29.8 %copy-start.18 = (f32[3,192]{1,0:T(4,128)S(1)}, f32[3,192]{1,0:T(4,128)}, u32[]{:S(2)}) copy-start(f32[3,192]{1,0:T(4,128)} %param.13) | copy-start | bytes 6916
  0.0 30.4 %copy-start.2 = (bf16[12,256,192]{1,2,0:T(8,128)(2,1)S(1)}, bf16[12,256,192]{1,2,0:T(8,128)(2,1)}, u32[]{:S(2)}) copy-start(bf16[12,256,192]{1,2,0:T(8,128)(2,1)} %param.9) | copy-start | bytes 3538948
  40.0 3.8 %copy-start.7 = (bf16[1,192,192]{2,0,1:T(2,128)(2,1)S(1)}, bf16[1,192,192]{2,0,1:T(2,128)(2,1)}, u32[]{:S(2)}) copy-start(bf16[1,192,192]{2,0,1:T(2,128)(2,1)} %get-tuple-element.118) | copy-start | bytes 221188
  64.7 2.9 copy-start.15
  67.6 2.4 copy-start.14
  67.6 2.9 copy-start.24
  70.6 0.9 copy-start.13
  70.6 2.0 copy-start.23
  72.6 0.9 copy-start.12
  72.6 2.0 copy-start.22
  74.5 1.9 copy-start.21
  76.4 1.9 copy-start.20
  82.6 9.4 %copy-start.6 = (bf16[1,192,192]{2,0,1:T(2,128)(2,1)S(1)}, bf16[1,192,192]{2,0,1:T(2,128)(2,1)}, u32[]{:S(2)}) copy-start(bf16[1,192,192]{2,0,1:T(2,128)(2,1)} %get-tuple-element.113) | copy-start | bytes 221188
  84.9 32.1 %all-to-all-start = ((bf16[12,128,2,192]{3,2,0,1:T(2,128)(2,1)}), bf16[12,128,2,192]{3,2,0,1:T(2,128)(2,1)S(1)}, u32[]{:S(2)}, u32[]{:S(2)}) async-start(bf16[12,128,2,192]{3,2,0,1:T(2,128)(2,1)} %copy.182), calls=%async_computation | async-start | bytes 3145728 | tf_op jit(solution)/shard_map/all_to_all | solution.py:138
  117.0 6.0 %copy-start = (bf16[12,128,2,192]{3,2,0,1:T(2,128)(2,1)}, bf16[12,128,2,192]{3,2,0,1:T(2,128)(2,1)S(1)}, u32[]{:S(2)}) copy-start(bf16[12,128,2,192]{3,2,0,1:T(2,128)(2,1)S(1)} %all-to-all-done) | copy-start | bytes 3538948
  123.1 5.4 %copy-start.10 = (bf16[1,192,192]{2,0,1:T(2,128)(2,1)S(1)}, bf16[1,192,192]{2,0,1:T(2,128)(2,1)}, u32[]{:S(2)}) copy-start(bf16[1,192,192]{2,0,1:T(2,128)(2,1)} %get-tuple-element.120) | copy-start | bytes 221188
  131.9 7.1 %copy-start.9 = (bf16[1,192,192]{2,0,1:T(2,128)(2,1)S(1)}, bf16[1,192,192]{2,0,1:T(2,128)(2,1)}, u32[]{:S(2)}) copy-start(bf16[1,192,192]{2,0,1:T(2,128)(2,1)} %get-tuple-element.119) | copy-start | bytes 221188
  142.3 7.0 %copy-start.8 = (bf16[1,192,192]{2,0,1:T(2,128)(2,1)S(1)}, bf16[1,192,192]{2,0,1:T(2,128)(2,1)}, u32[]{:S(2)}) copy-start(bf16[1,192,192]{2,0,1:T(2,128)(2,1)} %get-tuple-element.114) | copy-start | bytes 221188
  153.5 3.1 copy-start.5
  188.6 3.1 copy-start.5
  223.6 3.1 copy-start.5
  258.4 2.5 copy-start.1
  261.9 3.4 copy-start.11
  267.8 6.8 %copy-start.16 = (bf16[12,192]{1,0:T(8,128)(2,1)S(1)}, bf16[12,192]{1,0:T(8,128)(2,1)}, u32[]{:S(2)}) copy-start(bf16[12,192]{1,0:T(8,128)(2,1)} %param.12) | copy-start | bytes 13828
  267.8 46.0 %copy-start.17 = (bf16[6,384]{1,0:T(8,128)(2,1)S(1)}, bf16[6,384]{1,0:T(8,128)(2,1)}, u32[]{:S(2)}) copy-start(bf16[6,384]{1,0:T(8,128)(2,1)} %param.11) | copy-start | bytes 13828
  270.7 66.0 %all-to-all-start.1 = ((bf16[1536,1,2,192]{3,2,1,0:T(2,128)(2,1)}), bf16[1536,1,2,192]{3,2,1,0:T(2,128)(2,1)S(1)}, u32[]{:S(2)}, u32[]{:S(2)}) async-start(bf16[1536,1,2,192]{3,2,1,0:T(2,128)(2,1)} %copy.195), calls=%async_computation.1 | async-start | bytes 3145728 | tf_op jit(solution)/shard_map/all_to_all | solution.py:146
  354.2 5.6 %copy-start.3 = (f32[12,256,192]{2,1,0:T(8,128)S(1)}, f32[12,256,192]{2,1,0:T(8,128)}, u32[]{:S(2)}) copy-start(f32[12,256,192]{2,1,0:T(8,128)} %reshape.239) | copy-start | bytes 7077892
  358.3 3.7 copy-start.19
  362.0 5.6 %copy-start.4 = (f32[12,256,192]{1,2,0:T(8,128)S(1)}, f32[12,256,192]{1,2,0:T(8,128)}, u32[]{:S(2)}) copy-start(f32[12,256,192]{1,2,0:T(8,128)} %copy.203) | copy-start | bytes 7077892
where the time goes:
time: 378 us; the launch traced here: 371 us
  matrix products  143 us (38%)
  blocking collectives  89.6 us (24%)
  local copies, waits for them, and re-layouts  74.2 us (20%)
  other arithmetic  26.4 us (7%)
  waiting for transfers between devices  24.1 us (6%)
  starting transfers between devices  11 us (3%)
    sub x24, matrix products, softmax_rows(): exponent = jnp.exp(masked - row_maximum)  62.1 us
    dot_general x18, matrix products, one_block(): jnp.einsum('tdj,jtn->dtn', attention_probabilities, value_rows[..., train...  59.2 us
    all_gather x1, blocking collectives, local(): lax.all_gather(hidden_down_weight, 'fsdp', axis=0, tiled=True)  39.1 us
    all_gather x1, blocking collectives, local(): lax.all_gather(attn_weights, 'fsdp', axis=1, tiled=True)  27.7 us
    all_to_all x1, waiting for transfers between devices, local(): lax.all_to_all(split_cells, ('fsdp', 'feat'), split_axis=1, concat_axis=0...  24.1 us
    all_gather x1, blocking collectives, local(): lax.all_gather(hidden_up_weight, 'fsdp', axis=0, tiled=True)  22.8 us
    unnamed x55, local copies, waits for them, and re-layouts  18.9 us
    reshape x5, local copies, waits for them, and re-layouts, project(): product.astype(jnp.bfloat16).reshape(normed.shape[:-1] + (weight.shape[1],))  10.6 us
  transfers between devices with their start and end apart: 2, of which 1 were waited for; matrix products, arithmetic and copies ran while one was open for 0% of the time, Pallas kernels for 0%

commit v1 on v0

--- a/solution.py
+++ b/solution.py
@@ -2,6 +2,7 @@
 import jax.numpy as jnp
 from jax import lax
 from jax.sharding import PartitionSpec as P
+from jax.lax import all_to_all, psum
 
 HEADS = 6
 EPS = 1e-05
@@ -121,7 +122,15 @@
 ):
     weights, w_in, w_out = (
         lax.all_gather(attn_weights, "fsdp", axis=1, tiled=True),
-        lax.all_gather(hidden_up_weight, "fsdp", axis=0, tiled=True),
+        jnp.concatenate(
+            all_to_all(
+                jnp.stack([hidden_up_weight for _ in range(psum(1, "fsdp"))]),
+                split_axis=0,
+                axis_name="fsdp",
+                concat_axis=0,
+            ),
+            0,
+        ),
         lax.all_gather(hidden_down_weight, "fsdp", axis=0, tiled=True),
     )
     feat_live = jnp.arange(table_cells.shape[1]) < feature_count[0]

time: 378 us -> 363 us (0.960)
  blocking collectives: 89.6 us -> 66.7 us
  local copies, waits for them, and re-layouts: 74.2 us -> 83 us
  other arithmetic: 26.4 us -> 17.7 us
  starting transfers between devices: 11 us -> 19.4 us
    all_gather x1 -> x0, blocking collectives: 22.8 us -> none  [local(): lax.all_gather(hidden_up_weight, 'fsdp', axis=0, tiled=True)]
    convert_element_type x1 -> x3, local copies, waits for them, and re-layouts: 1.52 us -> 8.49 us  [normalize(): return (centered * lax.rsqrt(variance + EPS) * gain).astype(jnp.bfloat16)]
    reduce_sum x3, other arithmetic: 9.5 us -> 4.67 us  [normalize(): variance = jnp.mean(centered * centered, axis=-1, keepdims=True)]
    all_to_all x0 -> x1, starting transfers between devices: none -> 4.56 us  [local(): all_to_all(jnp.stack([hidden_up_weight for _ in range(psum(1, 'fsdp'))]),...]
    all_to_all x1, starting transfers between devices: 3.85 us -> 7.66 us  [local(): lax.all_to_all(at_owners, ('fsdp', 'feat'), split_axis=0, concat_axis=1,...]
    unnamed x55 -> x58, local copies, waits for them, and re-layouts: 18.9 us -> 20.8 us
  transfers between devices with their start and end apart: 2 -> 3, of which waited for: 1 -> 1; matrix products, arithmetic and copies ran while one was open for 0% -> 44% of each run, Pallas kernels for 0% -> 0%
where the time goes in v1:
time: 363 us; the launch traced here: 356 us
  matrix products  143 us (39%)
  local copies, waits for them, and re-layouts  83 us (23%)
  blocking collectives  66.7 us (18%)
  waiting for transfers between devices  24.2 us (7%)
  starting transfers between devices  19.4 us (5%)
  other arithmetic  17.7 us (5%)
    sub x24, matrix products, softmax_rows(): exponent = jnp.exp(masked - row_maximum)  62.1 us
    dot_general x18, matrix products, one_block(): jnp.einsum('tdj,jtn->dtn', attention_probabilities, value_rows[..., train...  59.1 us
    all_gather x1, blocking collectives, local(): lax.all_gather(hidden_down_weight, 'fsdp', axis=0, tiled=True)  39 us
    all_gather x1, blocking collectives, local(): lax.all_gather(attn_weights, 'fsdp', axis=1, tiled=True)  27.7 us
    all_to_all x1, waiting for transfers between devices, local(): lax.all_to_all(split_cells, ('fsdp', 'feat'), split_axis=1, concat_axis=0...  24.2 us
    unnamed x58, local copies, waits for them, and re-layouts  20.8 us
    convert_element_type x4, local copies, waits for them, and re-layouts, feed_forward(): value_rows.astype(jnp.float32)  13.3 us
    reshape x5, local copies, waits for them, and re-layouts, project(): product.astype(jnp.bfloat16).reshape(normed.shape[:-1] + (weight.shape[1],))  10.5 us
  transfers between devices with their start and end apart: 3, of which 1 were waited for; matrix products, arithmetic and copies ran while one was open for 44% of the time, Pallas kernels for 0%

profile of v1, /device:TPU:1, one launch (start us, length us, event | category | flops | bytes accessed | tf_op | source)
XLA Modules:
  0.0 355.7 jit_solution(428778431032061849)
XLA Ops:
  0.0 27.7 %all_gather.6 = bf16[8,192,192]{2,0,1:T(8,128)(2,1)S(1)} all-gather(bf16[8,6,192]{2,0,1:T(8,128)(2,1)} %param.10), channel_id=1, replica_groups=mesh['fsdp'=32,'feat'=4] {'fsdp'}, dimensions={1}, use_global_device_ids=true | all-gather | bytes 608256 | tf_op jit(solution)/shard_map/all_gather | solution.py:124
  27.7 2.2 fusion.408
  37.6 2.5 convolution_convert_fusion.3
  40.0 2.7 reshape.244
  43.9 3.1 fusion.406
  47.0 3.9 %fusion.410 = (f32[12,256]{1,0:T(8,128)S(1)}, f32[12,256,256]{1,2,0:T(8,128)}) fusion(pred[256]{0:T(512)(128)(4,1)S(1)} %iota_compare_fusion.1, bf16[12,256,32]{1,0,2:T(8,128)(2,1)} %get-tuple-element.136, bf16[12,256,32]{1,0,2:T(8,128)(2,1)} %get-tuple-element.106), kind=kOutput, calls=%fused_computation.349 | convolution fusion | flops 53477632 | bytes 3551488 | tf_op jit(solution)/shard_map/sub | solution.py:23
  50.9 4.0 %fusion.419 = (f32[12,256]{1,0:T(8,128)S(1)}, f32[12,256,256]{1,2,0:T(8,128)}) fusion(pred[256]{0:T(512)(128)(4,1)S(1)} %iota_compare_fusion.1, bf16[12,256,32]{1,0,2:T(8,128)(2,1)} %get-tuple-element.137, bf16[12,256,32]{1,0,2:T(8,128)(2,1)} %get-tuple-element.105), kind=kOutput, calls=%fused_computation.350 | convolution fusion | flops 53477632 | bytes 3551488 | tf_op jit(solution)/shard_map/sub | solution.py:23
  54.9 4.0 %fusion.428 = (f32[12,256]{1,0:T(8,128)S(1)}, f32[12,256,256]{1,2,0:T(8,128)}) fusion(pred[256]{0:T(512)(128)(4,1)S(1)} %iota_compare_fusion.1, bf16[12,256,32]{1,0,2:T(8,128)(2,1)} %get-tuple-element.138, bf16[12,256,32]{1,0,2:T(8,128)(2,1)} %get-tuple-element.104), kind=kOutput, calls=%fused_computation.351 | convolution fusion | flops 53477632 | bytes 3551488 | tf_op jit(solution)/shard_map/sub | solution.py:23
  58.9 2.9 fusion.437
  61.7 2.9 fusion.446
  64.7 2.9 fusion.455
  67.6 2.4 fusion.267
  82.6 2.2 copy.177
  84.8 7.2 %all-to-all-start = ((bf16[12,128,2,192]{3,2,0,1:T(2,128)(2,1)}), bf16[12,128,2,192]{3,2,0,1:T(2,128)(2,1)S(1)}, u32[]{:S(2)}, u32[]{:S(2)}) async-start(bf16[12,128,2,192]{3,2,0,1:T(2,128)(2,1)} %copy.177), calls=%async_computation | async-start | bytes 3145728 | tf_op jit(solution)/shard_map/all_to_all | solution.py:147
  92.8 24.2 %all-to-all-done = bf16[12,128,2,192]{3,2,0,1:T(2,128)(2,1)S(1)} async-done(((bf16[12,128,2,192]{3,2,0,1:T(2,128)(2,1)}), bf16[12,128,2,192]{3,2,0,1:T(2,128)(2,1)S(1)}, u32[]{:S(2)}, u32[]{:S(2)}) %all-to-all-start) | async-done | bytes 1179680 | tf_op jit(solution)/shard_map/all_to_all | solution.py:147
  117.7 4.6 %all-to-all-start.2 = ((bf16[32,6,384]{2,1,0:T(8,128)(2,1)}), bf16[32,6,384]{2,1,0:T(8,128)(2,1)}, u32[]{:S(2)}, u32[]{:S(2)}) async-start(bf16[32,6,384]{2,1,0:T(8,128)(2,1)} %stack.2), calls=%async_computation.2 | async-start | bytes 393216 | tf_op jit(solution)/shard_map/all_to_all | solution.py:126
  124.1 4.0 %multiply_reduce_fusion = f32[128,12,2]{2,1,0:T(8,128)S(1)} fusion(bf16[12,128,2,192]{3,2,0,1:T(2,128)(2,1)S(1)} %all-to-all-done, f32[128,12,2]{2,1,0:T(8,128)S(1)} %broadcast_multiply_fusion), kind=kLoop, calls=%fused_computation.187 | loop fusion | flops 2356224 | bytes 1204224 | tf_op jit(solution)/shard_map/reduce_sum | solution.py:16
  128.3 3.9 %multiply_convert_fusion = bf16[128,12,1,2,192]{4,3,1,0,2:T(2,128)(2,1)S(1)} fusion(bf16[12,128,2,192]{3,2,0,1:T(2,128)(2,1)S(1)} %all-to-all-done, f32[192]{0:T(256)S(1)} %bitcast.145, f32[128,12,2]{2,1,0:T(8,128)S(1)} %add_rsqrt_fusion, f32[128,12,2]{2,1,0:T(8,128)S(1)} %broadcast_multiply_fusion), kind=kLoop, calls=%fused_computation.186 | loop fusion | flops 2949120 | bytes 2384640 | tf_op jit(solution)/shard_map/convert_element_type | solution.py:17
  137.1 2.2 reshape.246
  139.3 4.9 %copy.185 = bf16[1536,2,192]{0,2,1:T(8,128)(2,1)} copy(bf16[1536,2,192]{2,1,0:T(2,128)(2,1)} %reshape.246) | data formatting | bytes 2359296
  147.5 2.2 reshape.247
  149.7 4.9 %copy.186 = bf16[1536,2,192]{0,2,1:T(8,128)(2,1)} copy(bf16[1536,2,192]{2,1,0:T(2,128)(2,1)} %reshape.247) | data formatting | bytes 2359296
  157.9 105.5 %while.11 = (s32[]{:T(128)}, bf16[3,512,2,192]{1,3,2,0:T(8,128)(2,1)}, bf16[3,512,2,192]{1,3,2,0:T(8,128)(2,1)S(1)}, bf16[1536,2,192]{0,2,1:T(8,128)(2,1)}, bf16...) while((s32[]{:T(128)}, bf16[3,512,2,192]{1,3,2,0:T(8,128)(2,1)}, ...), condition=%wide.region_29.30_spmd.clone, body=%wide.region_16.29_spmd.clone.sunk | while | flops 1897096704 | bytes 11085937 | solution.py:99
  158.8 3.1 fusion.547
  161.9 3.3 fusion.548
  165.2 2.1 fusion.549
  167.3 3.3 fusion.550
  172.8 3.3 fusion.552
  176.0 2.1 fusion.553
  178.2 3.3 fusion.554
  183.6 3.3 fusion.556
  186.9 2.1 fusion.557
  189.0 3.3 fusion.558
  193.8 3.1 fusion.547
  196.9 3.3 fusion.548
  200.2 2.1 fusion.549
  202.4 3.3 fusion.550
  207.8 3.3 fusion.552
  211.1 2.1 fusion.553
  213.2 3.3 fusion.554
  218.7 3.3 fusion.556
  224.1 3.3 fusion.558
  228.9 3.1 fusion.547
  232.0 3.3 fusion.548
  237.4 3.3 fusion.550
  242.8 3.3 fusion.552
  246.1 2.1 fusion.553
  248.3 3.3 fusion.554
  253.7 3.3 fusion.556
  259.1 3.3 fusion.558
  263.4 2.5 copy.230
  267.0 3.3 copy.189
  270.3 2.5 fusion.223
  272.8 2.9 copy.190
  275.7 7.7 %all-to-all-start.1 = ((bf16[1536,1,2,192]{3,2,1,0:T(2,128)(2,1)}), bf16[1536,1,2,192]{3,2,1,0:T(2,128)(2,1)S(1)}, u32[]{:S(2)}, u32[]{:S(2)}) async-start(bf16[1536,1,2,192]{3,2,1,0:T(2,128)(2,1)} %copy.190), calls=%async_computation.1 | async-start | bytes 3145728 | tf_op jit(solution)/shard_map/all_to_all | solution.py:155
  283.4 39.0 %all-gather = bf16[32,12,192]{2,1,0:T(8,128)(2,1)S(1)} all-gather(bf16[1,12,192]{2,1,0:T(8,128)(2,1)S(1)} %bitcast.142), channel_id=1, replica_groups=mesh['fsdp'=32,'feat'=4] {'fsdp'}, dimensions={0}, use_global_device_ids=true | all-gather | bytes 152064 | tf_op jit(solution)/shard_map/all_gather | solution.py:134
  326.0 3.8 %copy.191 = f32[128,12,1,2,192]{0,4,3,2,1:T(8,128)S(1)} copy(bf16[128,12,1,2,192]{4,3,1,0,2:T(2,128)(2,1)} %bitcast.138) | data formatting | bytes 3538944 | tf_op jit(solution)/shard_map/convert_element_type | solution.py:108
  331.0 2.9 copy.193
  333.8 4.1 %convert_element_type.222 = bf16[3072,192]{1,0:T(8,128)(2,1)} reshape(bf16[12,128,1,2,192]{4,3,1,0,2:T(2,128)(2,1)} %copy.193) | data formatting | bytes 2359296 | tf_op jit(solution)/shard_map/convert_element_type | solution.py:17
  337.9 3.4 copy.192
  341.3 3.9 %reshape.252 = f32[12,256,192]{2,1,0:T(8,128)S(1)} reshape(f32[12,128,1,2,192]{4,3,1,0,2:T(2,128)} %copy.192) | data formatting | bytes 4718592 | tf_op jit(solution)/shard_map/convert_element_type | solution.py:108
  345.2 2.2 copy.194
  347.4 5.0 %fusion.235 = f32[3072,192]{0,1:T(8,128)} fusion(bf16[384,192]{1,0:T(8,128)(2,1)S(1)} %copy-done.16, bf16[3072,192]{1,0:T(8,128)(2,1)} %convert_element_type.222, bf16[192,384]{1,0:T(8,128)(2,1)S(1)} %copy-done.17), kind=kOutput, calls=%fused_computation.225 | convolution fusion | flops 916586496 | bytes 3833856 | tf_op jit(solution)/shard_map/dot_general | solution.py:108
  352.4 2.9 fusion.234
  (123 shorter events, 65.1 us)
Async XLA Ops:
  0.0 29.8 %copy-start.21 = (f32[3,192]{1,0:T(4,128)S(1)}, f32[3,192]{1,0:T(4,128)}, u32[]{:S(2)}) copy-start(f32[3,192]{1,0:T(4,128)} %param.13) | copy-start | bytes 6916
  0.0 30.4 %copy-start.2 = (bf16[12,256,192]{1,2,0:T(8,128)(2,1)S(1)}, bf16[12,256,192]{1,2,0:T(8,128)(2,1)}, u32[]{:S(2)}) copy-start(bf16[12,256,192]{1,2,0:T(8,128)(2,1)} %param.9) | copy-start | bytes 3538948
  40.0 3.8 %copy-start.7 = (bf16[1,192,192]{2,0,1:T(2,128)(2,1)S(1)}, bf16[1,192,192]{2,0,1:T(2,128)(2,1)}, u32[]{:S(2)}) copy-start(bf16[1,192,192]{2,0,1:T(2,128)(2,1)} %get-tuple-element.118) | copy-start | bytes 221188
  64.7 2.9 copy-start.15
  67.6 2.4 copy-start.14
  67.6 2.9 copy-start.26
  70.5 0.9 copy-start.13
  70.5 2.0 copy-start.25
  72.5 0.9 copy-start.12
  72.5 2.0 copy-start.24
  74.5 1.9 copy-start.23
  76.4 1.9 copy-start.22
  82.6 9.5 %copy-start.6 = (bf16[1,192,192]{2,0,1:T(2,128)(2,1)S(1)}, bf16[1,192,192]{2,0,1:T(2,128)(2,1)}, u32[]{:S(2)}) copy-start(bf16[1,192,192]{2,0,1:T(2,128)(2,1)} %get-tuple-element.113) | copy-start | bytes 221188
  82.6 34.4 %copy-start.19 = (bf16[6,384]{1,0:T(8,128)(2,1)S(1)}, bf16[6,384]{1,0:T(8,128)(2,1)}, u32[]{:S(2)}) copy-start(bf16[6,384]{1,0:T(8,128)(2,1)} %param.11) | copy-start | bytes 13828
  84.8 32.1 %all-to-all-start = ((bf16[12,128,2,192]{3,2,0,1:T(2,128)(2,1)}), bf16[12,128,2,192]{3,2,0,1:T(2,128)(2,1)S(1)}, u32[]{:S(2)}, u32[]{:S(2)}) async-start(bf16[12,128,2,192]{3,2,0,1:T(2,128)(2,1)} %copy.177), calls=%async_computation | async-start | bytes 3145728 | tf_op jit(solution)/shard_map/all_to_all | solution.py:147
  117.0 11.3 %copy-start = (bf16[12,128,2,192]{3,2,0,1:T(2,128)(2,1)}, bf16[12,128,2,192]{3,2,0,1:T(2,128)(2,1)S(1)}, u32[]{:S(2)}) copy-start(bf16[12,128,2,192]{3,2,0,1:T(2,128)(2,1)S(1)} %all-to-all-done) | copy-start | bytes 3538948
  117.7 158.0 %all-to-all-start.2 = ((bf16[32,6,384]{2,1,0:T(8,128)(2,1)}), bf16[32,6,384]{2,1,0:T(8,128)(2,1)}, u32[]{:S(2)}, u32[]{:S(2)}) async-start(bf16[32,6,384]{2,1,0:T(8,128)(2,1)} %stack.2), calls=%async_computation.2 | async-start | bytes 393216 | tf_op jit(solution)/shard_map/all_to_all | solution.py:126
  128.3 5.4 %copy-start.10 = (bf16[1,192,192]{2,0,1:T(2,128)(2,1)S(1)}, bf16[1,192,192]{2,0,1:T(2,128)(2,1)}, u32[]{:S(2)}) copy-start(bf16[1,192,192]{2,0,1:T(2,128)(2,1)} %get-tuple-element.120) | copy-start | bytes 221188
  137.1 7.1 %copy-start.9 = (bf16[1,192,192]{2,0,1:T(2,128)(2,1)S(1)}, bf16[1,192,192]{2,0,1:T(2,128)(2,1)}, u32[]{:S(2)}) copy-start(bf16[1,192,192]{2,0,1:T(2,128)(2,1)} %get-tuple-element.119) | copy-start | bytes 221188
  147.5 7.0 %copy-start.8 = (bf16[1,192,192]{2,0,1:T(2,128)(2,1)S(1)}, bf16[1,192,192]{2,0,1:T(2,128)(2,1)}, u32[]{:S(2)}) copy-start(bf16[1,192,192]{2,0,1:T(2,128)(2,1)} %get-tuple-element.114) | copy-start | bytes 221188
  158.8 3.1 copy-start.5
  193.8 3.1 copy-start.5
  228.9 3.1 copy-start.5
  263.4 2.5 copy-start.1
  267.0 3.4 copy-start.11
  272.8 10.6 %copy-start.18 = (bf16[12,192]{1,0:T(8,128)(2,1)S(1)}, bf16[12,192]{1,0:T(8,128)(2,1)}, u32[]{:S(2)}) copy-start(bf16[12,192]{1,0:T(8,128)(2,1)} %param.12) | copy-start | bytes 13828
  275.7 49.1 %all-to-all-start.1 = ((bf16[1536,1,2,192]{3,2,1,0:T(2,128)(2,1)}), bf16[1536,1,2,192]{3,2,1,0:T(2,128)(2,1)S(1)}, u32[]{:S(2)}, u32[]{:S(2)}) async-start(bf16[1536,1,2,192]{3,2,1,0:T(2,128)(2,1)} %copy.190), calls=%async_computation.1 | async-start | bytes 3145728 | tf_op jit(solution)/shard_map/all_to_all | solution.py:155
  324.8 1.2 copy-start.4
  329.8 0.6 copy-start.20
  345.2 2.2 copy-start.16
  345.2 2.2 copy-start.17
  347.4 5.0 %copy-start.3 = (f32[12,256,192]{1,2,0:T(8,128)S(1)}, f32[12,256,192]{1,2,0:T(8,128)}, u32[]{:S(2)}) copy-start(f32[12,256,192]{1,2,0:T(8,128)} %copy.194) | copy-start | bytes 7077892
